TPU v7x, 256 devices: a whole 4x4x8 slice. The times are simulated.
256 devices in a mesh: ctx: 32 (over y, z), tp: 8 (over x, core).
Axes of the slice: x: 4, y: 4, z: 8, core: 2. Of those that a mesh axis runs over, the one named last changes fastest.
Arguments:
- context_block_rows: bfloat16 [16384, 8192], P('ctx', 'tp'), may hold values from -16 to 16
- query_hidden_rows: bfloat16 [64, 8192], P(None, 'tp'), may hold values from -16 to 16
- query_token_positions: int32 [64], replicated, may hold values from 16384 to 16573, as said below
- query_bound: int32 [64], replicated, may hold values from 1 to 16384, as said below
- query_matrix: bfloat16 [8192, 8192], P('ctx', 'tp'), may hold values from -0.0625 to 0.0625
- key_matrix: bfloat16 [8192, 1024], P('ctx', 'tp'), may hold values from -0.0625 to 0.0625
- value_matrix: bfloat16 [8192, 1024], P('ctx', 'tp'), may hold values from -0.0625 to 0.0625
Outputs:
- block_out: bfloat16 [16384, 8192], P('ctx', 'tp')
- query_out: bfloat16 [64, 8192], P(None, 'tp')
Inputs may be any that keep to these rules, and one draw needn't show every extreme that they name: query_token_positions rise strictly with the index; the first is 16384 and the last 16573. `query_bound`: some query token sees all 16384 context tokens.
All inputs are finite; a program needn't handle non-finite values.
Results may differ from a plain program's by a relative error of at most 0.0059.
The roundings to bfloat16 on the way count: a program that leaves them out, or rounds other values in their place, can miss the bound.
Values may be sent and summed in bfloat16 or wider, within the bound.
A program may use at most 128 MiB of HBM per device.

v0:
```python
import math
import jax
import jax.numpy as jnp
from jax import lax
from jax.sharding import PartitionSpec as P

HEAD_SIZE = 128


def from_root(value, axis, source):
    kept = jnp.where(lax.axis_index(axis) == source, value, 0).astype(value.dtype)
    return lax.psum(kept, axis)


def rope_table(half):
    values = []
    for index in range(half):
        freq = 500000.0 ** (-2.0 * index / (2.0 * half))
        wavelen = 2.0 * math.pi / freq
        if wavelen > 8192.0:
            values.append(freq / 8.0)
        elif wavelen < 2048.0:
            values.append(freq)
        else:
            smooth = (8192.0 / wavelen - 1.0) / 3.0
            values.append((1.0 - smooth) * freq / 8.0 + smooth * freq)
    return values


def apply_rotary(values, token_positions):
    half = values.shape[-1] // 2
    freqs = jnp.asarray(rope_table(half), jnp.float32)
    angle = token_positions.astype(jnp.float32)[:, None] * freqs[None, :]
    cosine = jnp.cos(angle)[:, None, :]
    sine = jnp.sin(angle)[:, None, :]
    first = values[..., :half]
    second = values[..., half:]
    return jnp.concatenate([first * cosine - second * sine, second * cosine + first * sine], -1)


def attend(query_heads_split, keys, values, valid):
    scale = 1.0 / math.sqrt(query_heads_split.shape[-1])
    scores = (
        jnp.einsum("qkgd,skd->qkgs", query_heads_split, keys, preferred_element_type=jnp.float32)
        * scale
    )
    scores = jnp.where(valid[:, None, None, :], scores, -1e30)
    peak = jnp.max(scores, -1)
    weights = jnp.exp(scores - peak[..., None])
    total = jnp.sum(weights, -1)
    mixed = jnp.einsum(
        "qkgs,skd->qkgd", weights.astype(jnp.bfloat16), values, preferred_element_type=jnp.float32
    )
    return (peak, total, mixed)


def on_device(
    context_block_rows,
    query_hidden_rows,
    query_token_positions,
    query_bound,
    query_matrix,
    key_matrix,
    value_matrix,
):
    ctx_index = lax.axis_index("ctx")
    blk = context_block_rows.shape[0]
    qcount = query_hidden_rows.shape[0]
    heads_q = query_matrix.shape[1] // HEAD_SIZE
    heads_kv = key_matrix.shape[1] // HEAD_SIZE
    head_group = heads_q // heads_kv
    whole_rows, whole_query = (
        lax.all_gather(context_block_rows, "tp", axis=1, tiled=True),
        lax.all_gather(query_hidden_rows, "tp", axis=1, tiled=True),
    )
    stacked = jnp.concatenate([whole_rows, whole_query], 0)
    head_rows = blk + qcount
    proj_query = jnp.dot(
        stacked,
        lax.all_gather(query_matrix, "ctx", axis=0, tiled=True),
        preferred_element_type=jnp.float32,
    )
    proj_key = jnp.dot(
        stacked,
        lax.all_gather(key_matrix, "ctx", axis=0, tiled=True),
        preferred_element_type=jnp.float32,
    )
    proj_value = jnp.dot(
        stacked,
        lax.all_gather(value_matrix, "ctx", axis=0, tiled=True),
        preferred_element_type=jnp.float32,
    )
    local_pos = ctx_index * blk + jnp.arange(blk, dtype=jnp.int32)
    k_block = apply_rotary(proj_key[:blk].reshape(blk, heads_kv, HEAD_SIZE), local_pos).astype(
        jnp.bfloat16
    )
    v_block = proj_value[:blk].reshape(blk, heads_kv, HEAD_SIZE).astype(jnp.bfloat16)
    key_token_rows = apply_rotary(
        proj_key[blk:head_rows].reshape(qcount, heads_kv, HEAD_SIZE), query_token_positions
    ).astype(jnp.bfloat16)
    value_token_rows = (
        proj_value[blk:head_rows].reshape(qcount, heads_kv, HEAD_SIZE).astype(jnp.bfloat16)
    )
    anchor_key, anchor_value = (from_root(k_block, "ctx", 0), from_root(v_block, "ctx", 0))
    q_block = apply_rotary(proj_query[:blk].reshape(blk, heads_q, HEAD_SIZE), local_pos).astype(
        jnp.bfloat16
    )
    query_token_rows = (
        apply_rotary(proj_query[blk:].reshape(qcount, heads_q, HEAD_SIZE), query_token_positions)
        .astype(jnp.bfloat16)
        .reshape(qcount, heads_kv, head_group, HEAD_SIZE)
    )
    keys_cat = jnp.concatenate([anchor_key, k_block], 0)
    values_cat = jnp.concatenate([anchor_value, v_block], 0)
    anchor_live = ctx_index > 0
    rows_step = min(blk, 512)
    rows_here = 0 + jnp.arange(rows_step, dtype=jnp.int32)
    valid = jnp.concatenate(
        [
            jnp.broadcast_to(anchor_live, (rows_step, blk)),
            rows_here[:, None] >= jnp.arange(blk, dtype=jnp.int32)[None, :],
        ],
        1,
    )
    query_heads_split = q_block.reshape(rows_step, heads_kv, head_group, HEAD_SIZE)
    peak, total, mixed = attend(query_heads_split, keys_cat, values_cat, valid)
    outputs = (
        (mixed / total[..., None]).astype(jnp.bfloat16).reshape(rows_step, heads_q * HEAD_SIZE)
    )
    valid_ctx = local_pos[None, :] < query_bound[:, None]
    peak, total, mixed = attend(query_token_rows, k_block, v_block, valid_ctx)
    top = lax.pmax(peak, "ctx")
    scaled = jnp.exp(peak - top)
    total_all, mixed_all = lax.psum((total * scaled, mixed * scaled[..., None]), "ctx")
    own = jnp.arange(qcount, dtype=jnp.int32)
    self_peak, self_total, self_mixed = attend(
        query_token_rows, key_token_rows, value_token_rows, own[:, None] >= own[None, :]
    )
    final = jnp.maximum(top, self_peak)
    w_ctx = jnp.exp(top - final)
    w_self = jnp.exp(self_peak - final)
    query_out = (mixed_all * w_ctx[..., None] + self_mixed * w_self[..., None]) / (
        total_all * w_ctx + self_total * w_self
    )[..., None]
    query_out = query_out.astype(jnp.bfloat16).reshape(qcount, heads_q * HEAD_SIZE)
    return (outputs, query_out)


def solution(mesh):
    placed = (
        P("ctx", "tp"),
        P(None, "tp"),
        P(),
        P(),
        P("ctx", "tp"),
        P("ctx", "tp"),
        P("ctx", "tp"),
    )
    return jax.shard_map(
        on_device,
        mesh=mesh,
        in_specs=placed,
        out_specs=(P("ctx", "tp"), P(None, "tp")),
        check_vma=False,
    )
```

profile of v0, /device:TPU:2, one launch (start us, length us, event | category | flops | bytes accessed | tf_op | source)
XLA Modules:
  0.0 689.7 jit_solution(3943614140132584248)
XLA Ops:
  7.2 0.7 all-gather.6.cloned.1.call-update
  7.9 0.7 all-gather.8.cloned.1.call-update
  8.7 0.7 all-gather.12.cloned.1.call-update
  9.4 0.5 all-gather.10.cloned.1.call-update
  10.0 0.5 all-gather.14.cloned.1.call-update
  10.6 0.7 convert_element_type.69
  11.3 0.1 iota_compare_fusion
  11.3 0.9 concatenate.62
  12.3 1.4 broadcast_compare_fusion
  13.6 0.8 multiply_cosine_fusion.3
  14.5 2.5 multiply_cosine_fusion
  17.0 47.3 %all-gather.6.cloned.1.call-done = bf16[512,8192]{1,0:T(8,128)(2,1)} async-done(((bf16[512,1024]{1,0:T(8,128)(2,1)}), bf16[512,8192]{1,0:T(8,128)(2,1)}) %all-gather.6.cloned.1.call-update) | async-done | bytes 8388624 | tf_op jit(solution)/shard_map/all_gather | solution.py:73
  64.3 7.6 %constant_dynamic-update-slice_fusion.1 = bf16[576,8192]{1,0:T(8,128)(2,1)} fusion(bf16[512,8192]{1,0:T(8,128)(2,1)} %all-gather.6.cloned.1.call-done), kind=kLoop, calls=%fused_computation.100 | loop fusion | bytes 16777216
  71.9 19.5 %all-gather.8.cloned.1.call-done = bf16[64,8192]{1,0:T(8,128)(2,1)} async-done(((bf16[64,1024]{1,0:T(8,128)(2,1)}), bf16[64,8192]{1,0:T(8,128)(2,1)}) %all-gather.8.cloned.1.call-update) | async-done | bytes 1048592 | tf_op jit(solution)/shard_map/all_gather | solution.py:74
  91.4 2.3 constant_dynamic-update-slice_fusion
  93.7 79.8 %all-gather.12.cloned.1.call-done = bf16[8192,128]{1,0:T(8,128)(2,1)} async-done(((bf16[256,128]{1,0:T(8,128)(2,1)}), bf16[8192,128]{1,0:T(8,128)(2,1)}) %all-gather.12.cloned.1.call-update) | async-done | bytes 2097168 | tf_op jit(solution)/shard_map/all_gather | solution.py:85
  173.5 5.8 fusion.83
  179.4 1.2 fusion.35
  180.6 0.8 maximum_select_fusion
  181.4 0.8 fusion.64
  182.2 68.9 %all-gather.10.cloned.1.call-done = bf16[8192,128]{1,0:T(8,128)(2,1)} async-done(((bf16[256,128]{1,0:T(8,128)(2,1)}), bf16[8192,128]{1,0:T(8,128)(2,1)}) %all-gather.10.cloned.1.call-update) | async-done | bytes 2097168 | tf_op jit(solution)/shard_map/all_gather | solution.py:90
  251.1 6.9 convolution_convert_fusion
  258.0 0.7 slice_bitcast_fusion.3
  258.9 132.5 %all-gather.14.cloned.1.call-done = bf16[8192,1024]{1,0:T(8,128)(2,1)} async-done(((bf16[256,1024]{1,0:T(8,128)(2,1)}), bf16[8192,1024]{1,0:T(8,128)(2,1)}) %all-gather.14.cloned.1.call-update) | async-done | bytes 16777232 | tf_op jit(solution)/shard_map/all_gather | solution.py:80
  391.4 14.9 %fusion.84 = f32[576,1024]{1,0:T(8,128)S(1)} fusion(bf16[576,8192]{1,0:T(8,128)(2,1)} %constant_dynamic-update-slice_fusion, bf16[8192,1024]{1,0:T(8,128)(2,1)} %all-gather.14.cloned.1.call-done), kind=kOutput, calls=%fused_computation.126 | convolution fusion | flops 9663676416 | bytes 28573696 | tf_op jit(solution)/shard_map/dot_general | solution.py:78
  406.4 0.1 slice_bitcast_fusion
  406.6 0.1 fusion.80
  406.7 0.1 subtract_convert_fusion.1
  406.8 1.4 fusion.81
  408.2 1.0 fusion.25
  409.1 71.4 %pmax.7 = f32[64,1,8]{0,2,1:T(8,128)S(1)} all-reduce(f32[64,1,8]{0,2,1:T(8,128)S(1)} %bitcast.169), channel_id=1, replica_groups=mesh['ctx'=32,'tp'=8] {'ctx'}, use_global_device_ids=true, to_apply=%region_5.6 | all-reduce | flops 512 | bytes 4096 | tf_op jit(solution)/shard_map/pmax | solution.py:132
  480.6 0.5 copy.38
  481.1 2.0 fusion.79
  483.1 0.6 bitcast_multiply_fusion.1
  483.7 1.1 fusion.14
  484.8 3.5 subtract_convert_fusion
  488.2 47.8 %all-reduce.7.cloned.1.call-done = (bf16[512,1,128]{2,0,1:T(8,128)(2,1)}, bf16[512,1,128]{2,0,1:T(8,128)(2,1)}) async-done(((bf16[512,1,128]{2,0,1:T(8,128)(2,1)}, bf16[512,1,128]{2,0,1:T(8,128)(2,1)}), (bf16[512,1,128]{2,0,1:T(8,128)(2,1)}, bf16[512,1,128]{2,0,1:T(8,128)(2,1)})) %all-reduce.7.cloned.1.call-update) | async-done | bytes 262160 | tf_op jit(solution)/shard_map/psum | solution.py:12
  536.1 10.7 %fusion.2 = (f32[512,8]{0,1:T(8,128)S(1)}, f32[1024,512,8]{1,0,2:T(8,128)}) fusion(pred[512,1024]{0,1:T(8,128)(4,1)} %concatenate.62, bf16[512,8,64]{2,0,1:T(8,128)(2,1)} %get-tuple-element.9, bf16[512,8,64]{2,0,1:T(8,128)(2,1)S(1)} %get-tuple-element.8, bf16[512,1,64]{2,0,1:T(8,128)(2,1)} %copy-done.1, bf16[512,1,64]{2,0,1:T(8,128)(2,1)S(1)} %get-tuple-element.14, ...), kind=kOutput, calls=%fused_computation.4 | convolution fusion | flops 1089204224 | bytes 18628608 | tf_op jit(solution)/shard_map/qkgd,skd->qkgs/dot_general | solution.py:44
  546.8 9.3 %fusion = f32[512,8]{0,1:T(8,128)S(1)} fusion(f32[1024,512,8]{1,0,2:T(8,128)} %get-tuple-element.32, f32[512,8]{0,1:T(8,128)S(1)} %get-tuple-element.31, pred[512,1024]{0,1:T(8,128)(4,1)S(1)} %copy-done), kind=kLoop, calls=%fused_computation.2 | loop fusion | flops 16773120 | bytes 17334272 | tf_op jit(solution)/shard_map/reduce_sum | solution.py:50
  556.1 0.3 fusion.82
  556.5 9.1 %fusion.7 = bf16[1,128,512,8]{2,1,3,0:T(8,128)(2,1)S(1)} fusion(f32[1024,512,8]{1,0,2:T(8,128)} %get-tuple-element.32, f32[512,8]{0,1:T(8,128)S(1)} %get-tuple-element.31, pred[512,1024]{0,1:T(8,128)(4,1)S(1)} %copy-done, f32[512,8]{0,1:T(8,128)S(1)} %fusion, bf16[512,1,128]{2,0,1:T(8,128)(2,1)S(1)} %copy-done.4, bf16[512,1,128]{2,0,1:T(8,128)(2,1)S(1)} %copy-done.10), kind=kOutput, calls=%fused_computation.10 | convolution fusion | flops 1092091904 | bytes 18644992 | tf_op jit(solution)/shard_map/qkgs,skd->qkgd/dot_general | solution.py:51
  565.6 0.1 fusion.44
  565.7 1.3 copy.29
  567.0 72.5 %psum.31 = f32[64,1,8]{0,2,1:T(8,128)S(1)} all-reduce(f32[64,1,8]{0,2,1:T(8,128)S(1)} %copy-done.8), channel_id=1, replica_groups=mesh['ctx'=32,'tp'=8] {'ctx'}, use_global_device_ids=true, to_apply=%region_9.10 | all-reduce | flops 512 | bytes 4096 | tf_op jit(solution)/shard_map/psum | solution.py:134
  639.5 41.2 %all-reduce.5.cloned.1.call-done = f32[64,1,8,128]{3,0,2,1:T(8,128)} async-done(((f32[64,1,8,128]{3,0,2,1:T(8,128)}), f32[64,1,8,128]{3,0,2,1:T(8,128)}) %all-reduce.5.cloned.1.call-update) | async-done | bytes 262160 | tf_op jit(solution)/shard_map/psum | solution.py:134
  680.7 1.3 fusion.19
  682.0 0.1 copy.28
  682.1 0.7 copy.50
  (39 shorter events, 0.5 us)
Async XLA Ops:
  7.2 57.1 %all-gather.6.cloned.1.call-start = ((), (), s32[]{:S(2)}) async-start(), calls=%async_computation | async-start | bytes 9437184 | tf_op jit(solution)/shard_map/all_gather | solution.py:73
  7.9 83.5 %all-gather.8.cloned.1.call-start = ((), (), s32[]{:S(2)}) async-start(), calls=%async_computation.1 | async-start | bytes 1179648 | tf_op jit(solution)/shard_map/all_gather | solution.py:74
  8.6 164.9 %all-gather.12.cloned.1.call-start = ((), (), s32[]{:S(2)}) async-start(), calls=%async_computation.3 | async-start | bytes 2162688 | tf_op jit(solution)/shard_map/all_gather | solution.py:85
  9.4 241.7 %all-gather.10.cloned.1.call-start = ((), (), s32[]{:S(2)}) async-start(), calls=%async_computation.2 | async-start | bytes 2162688 | tf_op jit(solution)/shard_map/all_gather | solution.py:90
  10.0 381.4 %all-gather.14.cloned.1.call-start = ((), (), s32[]{:S(2)}) async-start(), calls=%async_computation.4 | async-start | bytes 17301504 | tf_op jit(solution)/shard_map/all_gather | solution.py:80
  10.5 525.5 %all-reduce.7.cloned.1.call-start = ((), (), s32[]{:S(2)}) async-start(), calls=%async_computation.6 | async-start | bytes 524288 | tf_op jit(solution)/shard_map/psum | solution.py:12
  71.9 107.5 %copy-start.9 = (f32[64]{0:T(128)S(1)}, f32[64]{0:T(128)}, u32[]{:S(2)}) copy-start(f32[64]{0:T(128)} %constant.24.clone) | copy-start | bytes 772
  180.6 225.7 %copy-start.1 = (bf16[512,1,64]{2,0,1:T(8,128)(2,1)}, bf16[512,1,64]{2,0,1:T(8,128)(2,1)S(1)}, u32[]{:S(2)}) copy-start(bf16[512,1,64]{2,0,1:T(8,128)(2,1)S(1)} %get-tuple-element.15) | copy-start | bytes 196612
  258.0 133.4 %copy-start.2 = (bf16[576,128]{1,0:T(8,128)(2,1)}, bf16[576,128]{1,0:T(8,128)(2,1)S(1)}, u32[]{:S(2)}) copy-start(bf16[576,128]{1,0:T(8,128)(2,1)S(1)} %convolution_convert_fusion) | copy-start | bytes 442372
  258.8 421.9 %all-reduce.5.cloned.1.call-start = ((), (), s32[]{:S(2)}) async-start(), calls=%async_computation.5 | async-start | bytes 524288 | tf_op jit(solution)/shard_map/psum | solution.py:134
  480.6 2.5 copy-start.7
  480.6 3.1 copy-start.3
  536.1 10.7 %copy-start = (pred[512,1024]{0,1:T(8,128)(4,1)S(1)}, pred[512,1024]{0,1:T(8,128)(4,1)}, u32[]{:S(2)}) copy-start(pred[512,1024]{0,1:T(8,128)(4,1)} %concatenate.62) | copy-start | bytes 1572868
  546.8 9.3 %copy-start.5 = (bf16[64,64]{1,0:T(8,128)(2,1)S(1)}, bf16[64,64]{1,0:T(8,128)(2,1)}, u32[]{:S(2)}) copy-start(bf16[64,64]{1,0:T(8,128)(2,1)} %get-tuple-element.20) | copy-start | bytes 24580
  546.8 9.3 %copy-start.6 = (bf16[64,64]{1,0:T(8,128)(2,1)S(1)}, bf16[64,64]{1,0:T(8,128)(2,1)}, u32[]{:S(2)}) copy-start(bf16[64,64]{1,0:T(8,128)(2,1)} %get-tuple-element.21) | copy-start | bytes 24580
  546.8 9.6 %copy-start.4 = (bf16[512,1,128]{2,0,1:T(8,128)(2,1)S(1)}, bf16[512,1,128]{2,0,1:T(8,128)(2,1)}, u32[]{:S(2)}) copy-start(bf16[512,1,128]{2,0,1:T(8,128)(2,1)} %get-tuple-element.18) | copy-start | bytes 393220
  546.8 9.6 %copy-start.10 = (bf16[512,1,128]{2,0,1:T(8,128)(2,1)S(1)}, bf16[512,1,128]{2,0,1:T(8,128)(2,1)}, u32[]{:S(2)}) copy-start(bf16[512,1,128]{2,0,1:T(8,128)(2,1)} %get-tuple-element.7) | copy-start | bytes 393220
  556.5 10.5 %copy-start.8 = (f32[64,1,8]{0,2,1:T(8,128)S(1)}, f32[64,1,8]{0,2,1:T(8,128)}, u32[]{:S(2)}) copy-start(f32[64,1,8]{0,2,1:T(8,128)} %get-tuple-element.25) | copy-start | bytes 6148
Sparse Core Ops, SparseCore 0:
  9.8 54.4 all-gather.5
  66.1 25.2 all-gather.7
  94.0 79.4 all-gather.11
  176.0 75.1 all-gather.9
  253.6 137.7 all-gather.13
  394.7 141.2 all-reduce.6
  539.5 141.1 all-reduce.4
where the time goes:
time: 690 us
  waiting for transfers between devices  440 us (64%)
  blocking collectives  144 us (21%)
  matrix products  51.5 us (7%)
  other arithmetic  23.5 us (3%)
  local copies, waits for them, and re-layouts  15.8 us (2%)
  between operations  14.4 us (2%)
    all_gather x1, waiting for transfers between devices, on_device(): lax.all_gather(query_matrix, 'ctx', axis=0, tiled=True)  133 us
    all_gather x1, waiting for transfers between devices, on_device(): lax.all_gather(key_matrix, 'ctx', axis=0, tiled=True)  79.8 us
    psum x1, blocking collectives, on_device(): lax.psum((total * scaled, mixed * scaled[..., None]), 'ctx')  72.5 us
    pmax x1, blocking collectives, on_device(): top = lax.pmax(peak, 'ctx')  71.4 us
    all_gather x1, waiting for transfers between devices, on_device(): lax.all_gather(value_matrix, 'ctx', axis=0, tiled=True)  68.9 us
    psum x1, waiting for transfers between devices, from_root(): return lax.psum(kept, axis)  47.8 us
    all_gather x1, waiting for transfers between devices, on_device(): lax.all_gather(context_block_rows, 'tp', axis=1, tiled=True)  47.3 us
    psum x1, waiting for transfers between devices, on_device(): lax.psum((total * scaled, mixed * scaled[..., None]), 'ctx')  41.2 us
  transfers between devices with their start and end apart: 7, of which 7 were waited for; matrix products, arithmetic and copies ran while one was open for 13% of the time, Pallas kernels for 0%

commit v1 on v0

--- a/solution.py
+++ b/solution.py
@@ -5,6 +5,28 @@
 from jax.sharding import PartitionSpec as P
 
 HEAD_SIZE = 128
+
+
+def joined_along(parts, dim):
+    parts = jnp.moveaxis(parts, 0, dim)
+    shape = parts.shape
+    return parts.reshape(*shape[:dim], shape[dim] * shape[dim + 1], *shape[dim + 2 :])
+
+
+def gather_around(value, axis, dim):
+    size = lax.axis_size(axis)
+    pairs = [(i, (i + 1) % size) for i in range(size)]
+    back = [(b, a) for a, b in pairs]
+    lower, upper = ([], [])
+    for hop in range(size - 1):
+        if hop % 2 == 0:
+            lower.append(lax.ppermute(lower[-1] if lower else value, axis, pairs))
+        else:
+            upper.append(lax.ppermute(upper[-1] if upper else value, axis, back))
+    blocks = jnp.stack([*lower[::-1], value, *upper])
+    shift = lax.axis_index(axis) - len(lower)
+    blocks = blocks[(jnp.arange(size) - shift) % size]
+    return joined_along(blocks, dim)
 
 
 def from_root(value, axis, source):
@@ -71,7 +93,7 @@
     head_group = heads_q // heads_kv
     whole_rows, whole_query = (
         lax.all_gather(context_block_rows, "tp", axis=1, tiled=True),
-        lax.all_gather(query_hidden_rows, "tp", axis=1, tiled=True),
+        gather_around(query_hidden_rows, "tp", 1),
     )
     stacked = jnp.concatenate([whole_rows, whole_query], 0)
     head_rows = blk + qcount

time: 690 us -> 664 us (0.962)
  waiting for transfers between devices: 440 us -> 409 us
    all_gather x1 -> x0, waiting for transfers between devices: 19.5 us -> none  [on_device(): lax.all_gather(query_hidden_rows, 'tp', axis=1, tiled=True)]
    all_gather x1, waiting for transfers between devices: 47.3 us -> 32.6 us  [on_device(): lax.all_gather(context_block_rows, 'tp', axis=1, tiled=True)]
    ppermute x0 -> x7, waiting for transfers between devices: none -> 9.7 us  [the longest x4 9.69 us: gather_around(): lower.append(lax.ppermute(lower[-1] if lower else value, axis, pairs))]
  transfers between devices with their start and end apart: 7 -> 13, of which waited for: 7 -> 9; matrix products, arithmetic and copies ran while one was open for 13% -> 13% of each run, Pallas kernels for 0% -> 0%
where the time goes in v1:
time: 664 us
  waiting for transfers between devices  409 us (62%)
  blocking collectives  144 us (22%)
  matrix products  51.5 us (8%)
  other arithmetic  23.5 us (4%)
  local copies, waits for them, and re-layouts  16.3 us (2%)
  between operations  14.5 us (2%)
    all_gather x1, waiting for transfers between devices, on_device(): lax.all_gather(query_matrix, 'ctx', axis=0, tiled=True)  133 us
    all_gather x1, waiting for transfers between devices, on_device(): lax.all_gather(key_matrix, 'ctx', axis=0, tiled=True)  73.3 us
    psum x1, blocking collectives, on_device(): lax.psum((total * scaled, mixed * scaled[..., None]), 'ctx')  72.5 us
    pmax x1, blocking collectives, on_device(): top = lax.pmax(peak, 'ctx')  71.4 us
    all_gather x1, waiting for transfers between devices, on_device(): lax.all_gather(value_matrix, 'ctx', axis=0, tiled=True)  69.1 us
    psum x1, waiting for transfers between devices, from_root(): return lax.psum(kept, axis)  47.8 us
    psum x1, waiting for transfers between devices, on_device(): lax.psum((total * scaled, mixed * scaled[..., None]), 'ctx')  41.1 us
    all_gather x1, waiting for transfers between devices, on_device(): lax.all_gather(context_block_rows, 'tp', axis=1, tiled=True)  32.6 us
  transfers between devices with their start and end apart: 13, of which 9 were waited for; matrix products, arithmetic and copies ran while one was open for 13% of the time, Pallas kernels for 0%

profile of v1, /device:TPU:2, one launch (start us, length us, event | category | flops | bytes accessed | tf_op | source)
XLA Modules:
  0.0 663.9 jit_solution(9031458284458859280)
XLA Ops:
  7.2 0.7 all-gather.5.cloned.1.call-update
  7.9 0.7 all-gather.9.cloned.1.call-update
  8.7 0.7 all-gather.7.cloned.1.call-update
  9.4 0.5 all-gather.11.cloned.1.call-update
  10.0 1.7 collective-permute-start.4
  11.8 0.7 convert_element_type.69
  12.4 2.5 multiply_cosine_fusion
  14.9 0.8 multiply_cosine_fusion.3
  15.8 1.4 broadcast_compare_fusion
  17.2 3.0 collective-permute-done.1
  20.3 1.8 collective-permute-start.5
  22.0 2.5 collective-permute-done.2
  24.6 0.9 concatenate.62
  25.5 1.7 collective-permute-start.6
  27.2 4.1 collective-permute-done.3
  31.4 0.9 bitcast_dynamic-update-slice_fusion.3
  32.4 0.6 gather_fusion
  33.1 32.6 %all-gather.5.cloned.1.call-done = bf16[512,8192]{1,0:T(8,128)(2,1)} async-done(((bf16[512,1024]{1,0:T(8,128)(2,1)}), bf16[512,8192]{1,0:T(8,128)(2,1)}) %all-gather.5.cloned.1.call-update) | async-done | bytes 8388624 | tf_op jit(solution)/shard_map/all_gather | solution.py:95
  65.7 7.6 %constant_dynamic-update-slice_fusion.1 = bf16[576,8192]{1,0:T(8,128)(2,1)} fusion(bf16[512,8192]{1,0:T(8,128)(2,1)} %all-gather.5.cloned.1.call-done), kind=kLoop, calls=%fused_computation.103 | loop fusion | bytes 16777216
  73.3 1.1 constant_dynamic-update-slice_fusion
  74.4 73.3 %all-gather.9.cloned.1.call-done = bf16[8192,128]{1,0:T(8,128)(2,1)} async-done(((bf16[256,128]{1,0:T(8,128)(2,1)}), bf16[8192,128]{1,0:T(8,128)(2,1)}) %all-gather.9.cloned.1.call-update) | async-done | bytes 2097168 | tf_op jit(solution)/shard_map/all_gather | solution.py:107
  147.7 5.8 fusion.85
  153.6 1.2 fusion.35
  154.8 0.8 maximum_select_fusion
  155.6 0.8 fusion.64
  156.4 69.1 %all-gather.7.cloned.1.call-done = bf16[8192,128]{1,0:T(8,128)(2,1)} async-done(((bf16[256,128]{1,0:T(8,128)(2,1)}), bf16[8192,128]{1,0:T(8,128)(2,1)}) %all-gather.7.cloned.1.call-update) | async-done | bytes 2097168 | tf_op jit(solution)/shard_map/all_gather | solution.py:112
  225.5 6.9 %convolution_convert_fusion = bf16[576,128]{1,0:T(8,128)(2,1)S(1)} fusion(bf16[576,8192]{1,0:T(8,128)(2,1)} %constant_dynamic-update-slice_fusion, bf16[8192,128]{1,0:T(8,128)(2,1)} %all-gather.7.cloned.1.call-done), kind=kOutput, calls=%fused_computation.27 | convolution fusion | flops 1208033280 | bytes 11681792 | tf_op jit(solution)/shard_map/dot_general | solution.py:110
  232.4 0.8 slice_bitcast_fusion.3
  233.2 132.5 %all-gather.11.cloned.1.call-done = bf16[8192,1024]{1,0:T(8,128)(2,1)} async-done(((bf16[256,1024]{1,0:T(8,128)(2,1)}), bf16[8192,1024]{1,0:T(8,128)(2,1)}) %all-gather.11.cloned.1.call-update) | async-done | bytes 16777232 | tf_op jit(solution)/shard_map/all_gather | solution.py:102
  365.8 14.9 %fusion.86 = f32[576,1024]{1,0:T(8,128)S(1)} fusion(bf16[576,8192]{1,0:T(8,128)(2,1)} %constant_dynamic-update-slice_fusion, bf16[8192,1024]{1,0:T(8,128)(2,1)} %all-gather.11.cloned.1.call-done), kind=kOutput, calls=%fused_computation.142 | convolution fusion | flops 9663676416 | bytes 28573696 | tf_op jit(solution)/shard_map/dot_general | solution.py:100
  381.2 1.4 fusion.83
  382.6 1.0 fusion.25
  383.5 71.4 %pmax.7 = f32[64,1,8]{0,2,1:T(8,128)S(1)} all-reduce(f32[64,1,8]{0,2,1:T(8,128)S(1)} %bitcast.192), channel_id=1, replica_groups=mesh['ctx'=32,'tp'=8] {'ctx'}, use_global_device_ids=true, to_apply=%region_5.6 | all-reduce | flops 512 | bytes 4096 | tf_op jit(solution)/shard_map/pmax | solution.py:154
  455.0 0.5 copy.40
  455.5 2.0 fusion.81
  457.5 0.6 bitcast_multiply_fusion.1
  458.1 1.1 fusion.14
  459.1 3.5 subtract_convert_fusion
  462.6 47.8 %all-reduce.7.cloned.1.call-done = (bf16[512,1,128]{2,0,1:T(8,128)(2,1)}, bf16[512,1,128]{2,0,1:T(8,128)(2,1)}) async-done(((bf16[512,1,128]{2,0,1:T(8,128)(2,1)}, bf16[512,1,128]{2,0,1:T(8,128)(2,1)}), (bf16[512,1,128]{2,0,1:T(8,128)(2,1)}, bf16[512,1,128]{2,0,1:T(8,128)(2,1)})) %all-reduce.7.cloned.1.call-update) | async-done | bytes 262160 | tf_op jit(solution)/shard_map/psum | solution.py:34
  510.4 10.7 %fusion.2 = (f32[512,8]{0,1:T(8,128)S(1)}, f32[1024,512,8]{1,0,2:T(8,128)}) fusion(pred[512,1024]{0,1:T(8,128)(4,1)} %concatenate.62, bf16[512,8,64]{2,0,1:T(8,128)(2,1)} %get-tuple-element.9, bf16[512,8,64]{2,0,1:T(8,128)(2,1)S(1)} %get-tuple-element.8, bf16[512,1,64]{2,0,1:T(8,128)(2,1)} %copy-done.1, bf16[512,1,64]{2,0,1:T(8,128)(2,1)S(1)} %get-tuple-element.14, ...), kind=kOutput, calls=%fused_computation.5 | convolution fusion | flops 1089204224 | bytes 18628608 | tf_op jit(solution)/shard_map/qkgd,skd->qkgs/dot_general | solution.py:66
  521.2 9.3 %fusion = f32[512,8]{0,1:T(8,128)S(1)} fusion(f32[1024,512,8]{1,0,2:T(8,128)} %get-tuple-element.32, f32[512,8]{0,1:T(8,128)S(1)} %get-tuple-element.31, pred[512,1024]{0,1:T(8,128)(4,1)S(1)} %copy-done), kind=kLoop, calls=%fused_computation.3 | loop fusion | flops 16773120 | bytes 17334272 | tf_op jit(solution)/shard_map/reduce_sum | solution.py:72
  530.4 0.3 fusion.84
  530.8 9.1 %fusion.7 = bf16[1,128,512,8]{2,1,3,0:T(8,128)(2,1)S(1)} fusion(f32[1024,512,8]{1,0,2:T(8,128)} %get-tuple-element.32, f32[512,8]{0,1:T(8,128)S(1)} %get-tuple-element.31, pred[512,1024]{0,1:T(8,128)(4,1)S(1)} %copy-done, f32[512,8]{0,1:T(8,128)S(1)} %fusion, bf16[512,1,128]{2,0,1:T(8,128)(2,1)S(1)} %copy-done.4, bf16[512,1,128]{2,0,1:T(8,128)(2,1)S(1)} %copy-done.10), kind=kOutput, calls=%fused_computation.11 | convolution fusion | flops 1092091904 | bytes 18644992 | tf_op jit(solution)/shard_map/qkgs,skd->qkgd/dot_general | solution.py:73
  540.0 1.3 copy.30
  541.3 72.5 %psum.31 = f32[64,1,8]{0,2,1:T(8,128)S(1)} all-reduce(f32[64,1,8]{0,2,1:T(8,128)S(1)} %copy-done.8), channel_id=1, replica_groups=mesh['ctx'=32,'tp'=8] {'ctx'}, use_global_device_ids=true, to_apply=%region_9.10 | all-reduce | flops 512 | bytes 4096 | tf_op jit(solution)/shard_map/psum | solution.py:156
  613.9 41.1 %all-reduce.5.cloned.1.call-done = f32[64,1,8,128]{3,0,2,1:T(8,128)} async-done(((f32[64,1,8,128]{3,0,2,1:T(8,128)}), f32[64,1,8,128]{3,0,2,1:T(8,128)}) %all-reduce.5.cloned.1.call-update) | async-done | bytes 262160 | tf_op jit(solution)/shard_map/psum | solution.py:156
  655.0 1.3 fusion.19
  656.4 0.7 copy.52
  (62 shorter events, 1.3 us)
Async XLA Ops:
  7.2 58.5 %all-gather.5.cloned.1.call-start = ((), (), s32[]{:S(2)}) async-start(), calls=%async_computation | async-start | bytes 9437184 | tf_op jit(solution)/shard_map/all_gather | solution.py:95
  7.9 139.8 %all-gather.9.cloned.1.call-start = ((), (), s32[]{:S(2)}) async-start(), calls=%async_computation.2 | async-start | bytes 2162688 | tf_op jit(solution)/shard_map/all_gather | solution.py:107
  8.6 216.8 %all-gather.7.cloned.1.call-start = ((), (), s32[]{:S(2)}) async-start(), calls=%async_computation.1 | async-start | bytes 2162688 | tf_op jit(solution)/shard_map/all_gather | solution.py:112
  9.4 356.4 %all-gather.11.cloned.1.call-start = ((), (), s32[]{:S(2)}) async-start(), calls=%async_computation.3 | async-start | bytes 17301504 | tf_op jit(solution)/shard_map/all_gather | solution.py:102
  10.0 500.5 %all-reduce.7.cloned.1.call-start = ((), (), s32[]{:S(2)}) async-start(), calls=%async_computation.5 | async-start | bytes 524288 | tf_op jit(solution)/shard_map/psum | solution.py:34
  10.0 5.8 collective-permute-start
  10.0 10.2 %collective-permute-start.4 = (bf16[64,1024]{1,0:T(8,128)(2,1)}, bf16[64,1024]{1,0:T(8,128)(2,1)S(1)}, u32[]{:S(2)}, u32[]{:S(2)}) collective-permute-start(bf16[64,1024]{1,0:T(8,128)(2,1)} %param.12), channel_id=1, source_target_pairs={{1,0},{2,1},{3,2},{4,3},{5,4},{6,5},{7,6},{0,7},{9,8},{10,9},{11,1... | collective-permute-start | bytes 393224 | tf_op jit(solution)/shard_map/ppermute | solution.py:25
  15.8 4.4 collective-permute-start.1
  20.2 4.4 collective-permute-start.2
  20.3 5.2 collective-permute-start.5
  24.6 6.8 %collective-permute-start.3 = (bf16[64,1024]{1,0:T(8,128)(2,1)S(1)}, bf16[64,1024]{1,0:T(8,128)(2,1)S(1)}, u32[]{:S(2)}, u32[]{:S(2)}) collective-permute-start(bf16[64,1024]{1,0:T(8,128)(2,1)S(1)} %collective-permute-done.2), channel_id=1, source_target_pairs={{0,1},{1,2},{2,3},{3,4},{4,5},{5,6},{6,7},{7,0},{8,9},{9,10},{10,1... | collective-permute-start | bytes 393224 | tf_op jit(solution)/shard_map/ppermute | solution.py:23
  25.5 6.9 %collective-permute-start.6 = (bf16[64,1024]{1,0:T(8,128)(2,1)S(1)}, bf16[64,1024]{1,0:T(8,128)(2,1)S(1)}, u32[]{:S(2)}, u32[]{:S(2)}) collective-permute-start(bf16[64,1024]{1,0:T(8,128)(2,1)S(1)} %collective-permute-done.5), channel_id=1, source_target_pairs={{1,0},{2,1},{3,2},{4,3},{5,4},{6,5},{7,6},{0,7},{9,8},{10,9},{11,1... | collective-permute-start | bytes 393224 | tf_op jit(solution)/shard_map/ppermute | solution.py:25
  73.3 80.3 %copy-start.9 = (f32[64]{0:T(128)S(1)}, f32[64]{0:T(128)}, u32[]{:S(2)}) copy-start(f32[64]{0:T(128)} %constant.46.clone) | copy-start | bytes 772
  154.8 225.9 %copy-start.1 = (bf16[512,1,64]{2,0,1:T(8,128)(2,1)}, bf16[512,1,64]{2,0,1:T(8,128)(2,1)S(1)}, u32[]{:S(2)}) copy-start(bf16[512,1,64]{2,0,1:T(8,128)(2,1)S(1)} %get-tuple-element.15) | copy-start | bytes 196612
  232.4 133.4 %copy-start.2 = (bf16[576,128]{1,0:T(8,128)(2,1)}, bf16[576,128]{1,0:T(8,128)(2,1)S(1)}, u32[]{:S(2)}) copy-start(bf16[576,128]{1,0:T(8,128)(2,1)S(1)} %convolution_convert_fusion) | copy-start | bytes 442372
  233.2 421.8 %all-reduce.5.cloned.1.call-start = ((), (), s32[]{:S(2)}) async-start(), calls=%async_computation.4 | async-start | bytes 524288 | tf_op jit(solution)/shard_map/psum | solution.py:156
  455.0 2.5 copy-start.7
  455.0 3.1 copy-start.3
  510.4 10.7 %copy-start = (pred[512,1024]{0,1:T(8,128)(4,1)S(1)}, pred[512,1024]{0,1:T(8,128)(4,1)}, u32[]{:S(2)}) copy-start(pred[512,1024]{0,1:T(8,128)(4,1)} %concatenate.62) | copy-start | bytes 1572868
  521.1 9.3 %copy-start.5 = (bf16[64,64]{1,0:T(8,128)(2,1)S(1)}, bf16[64,64]{1,0:T(8,128)(2,1)}, u32[]{:S(2)}) copy-start(bf16[64,64]{1,0:T(8,128)(2,1)} %get-tuple-element.20) | copy-start | bytes 24580
  521.1 9.3 %copy-start.6 = (bf16[64,64]{1,0:T(8,128)(2,1)S(1)}, bf16[64,64]{1,0:T(8,128)(2,1)}, u32[]{:S(2)}) copy-start(bf16[64,64]{1,0:T(8,128)(2,1)} %get-tuple-element.21) | copy-start | bytes 24580
  521.1 9.6 %copy-start.4 = (bf16[512,1,128]{2,0,1:T(8,128)(2,1)S(1)}, bf16[512,1,128]{2,0,1:T(8,128)(2,1)}, u32[]{:S(2)}) copy-start(bf16[512,1,128]{2,0,1:T(8,128)(2,1)} %get-tuple-element.18) | copy-start | bytes 393220
  521.1 9.6 %copy-start.10 = (bf16[512,1,128]{2,0,1:T(8,128)(2,1)S(1)}, bf16[512,1,128]{2,0,1:T(8,128)(2,1)}, u32[]{:S(2)}) copy-start(bf16[512,1,128]{2,0,1:T(8,128)(2,1)} %get-tuple-element.7) | copy-start | bytes 393220
  530.8 10.5 %copy-start.8 = (f32[64,1,8]{0,2,1:T(8,128)S(1)}, f32[64,1,8]{0,2,1:T(8,128)}, u32[]{:S(2)}) copy-start(f32[64,1,8]{0,2,1:T(8,128)} %get-tuple-element.25) | copy-start | bytes 6148
Sparse Core Ops, SparseCore 0:
  9.8 55.8 all-gather.4
  68.3 79.3 all-gather.8
  150.3 75.1 all-gather.6
  227.9 137.7 all-gather.10
  369.1 141.2 all-reduce.6
  513.8 141.1 all-reduce.4
